TPU v7x, 32 devices: a whole 2x2x4 slice. The times are simulated.
32 devices in a mesh: group: 2 (over x), ctx: 8 (over z, y), dp: 2 (over core).
Axes of the slice: x: 2, y: 2, z: 4, core: 2. Of those that a mesh axis runs over, the one named last changes fastest.
Arguments:
- tokens: bfloat16 [16384, 5120], P(('group', 'ctx')), parts along dimension 0, may hold values from -6 to 6
- cotangent: bfloat16 [16384, 1024], P(('group', 'ctx')), parts along dimension 0, may hold values from -0.1875 to 0.1875
- factor_a: float32 [512, 5120], P(('group', 'ctx')), parts along dimension 0, may hold values from -0.078125 to 0.078125
- factor_b: float32 [512, 1024], P(('group', 'ctx')), parts along dimension 0, may hold values from -0.1875 to 0.1875
- moment_a: float32 [512, 5120], P(('group', 'ctx', 'dp')), parts along dimension 0, may hold values from -3 to 3
- moment_b: float32 [512, 1024], P(('group', 'ctx', 'dp')), parts along dimension 0, may hold values from -3 to 3
- second_a: float32 [512, 5120], P(('group', 'ctx', 'dp')), parts along dimension 0, may hold values from 0.1 to 2
- second_b: float32 [512, 1024], P(('group', 'ctx', 'dp')), parts along dimension 0, may hold values from 0.1 to 2
- token_counts: int32 [16], P('group'), parts along dimension 0, may hold values from 1 to 2048, 8192 in all
- rank_blocks: int32 [16], P('group'), parts along dimension 0, may hold values from 1 to 16, 32 in all
Outputs:
- new_factor_a: float32 [512, 5120], P(('group', 'ctx')), parts along dimension 0
- new_factor_b: float32 [512, 1024], P(('group', 'ctx')), parts along dimension 0
- new_moment_a: float32 [512, 5120], P(('group', 'ctx', 'dp')), parts along dimension 0
- new_second_a: float32 [512, 5120], P(('group', 'ctx', 'dp')), parts along dimension 0
- new_moment_b: float32 [512, 1024], P(('group', 'ctx', 'dp')), parts along dimension 0
- new_second_b: float32 [512, 1024], P(('group', 'ctx', 'dp')), parts along dimension 0
There are 2 independent parts, one for each index of `group`. A program takes and returns all parts, laid end to end along the dimension named above; each array names one. Nothing has to cross between parts.
Inputs may be any that keep to these rules, and one draw needn't show every extreme that they name: `token_counts`: the tenants' token segments fill the batch of 8192 tokens; the largest holds exactly 2048 tokens. The ranks 8 * rank_blocks sum to 256; the largest rank is exactly 128.
All inputs are finite; a program needn't handle non-finite values.
Results may differ from a plain program's by a relative error of at most 0.00088.
Values may be sent and summed in bfloat16 or wider, within the bound.
A program may use at most 64 MiB of HBM per device.

v0:
```python
import jax
import jax.numpy as jnp
from jax import lax
from jax.sharding import PartitionSpec as P

beta_one = 0.9
beta_two = 0.95
bias_one = 1.0 - 0.9**10
bias_two = 1.0 - 0.95**10
learn_rate = 0.01
decay_rate = 0.1
epsilon = 1e-08


def tenant_of(positions, ends):
    return jnp.sum((positions[:, None] >= ends[None, :]).astype(jnp.int32), axis=1)


def adamw(param, grad, moment, second):
    new_moment = beta_one * moment + (1.0 - beta_one) * grad
    new_second = beta_two * second + (1.0 - beta_two) * grad * grad
    update = new_moment / bias_one / (jnp.sqrt(new_second / bias_two) + epsilon)
    return (param - learn_rate * (update + decay_rate * param), new_moment, new_second)


def partial_grads(
    token_rows, grad_rows, low_a, low_b, positions, rank_rows, token_counts, rank_ends
):
    token_tenant = tenant_of(positions, jnp.cumsum(token_counts))
    row_tenant = tenant_of(rank_rows, rank_ends)
    same_tenant = token_tenant[:, None] == row_tenant[None, :]
    contract = (((1,), (1,)), ((), ()))
    scores_a = lax.dot_general(token_rows, low_a, contract, preferred_element_type=jnp.float32)
    scores_b = lax.dot_general(grad_rows, low_b, contract, preferred_element_type=jnp.float32)
    hidden = jnp.where(same_tenant, scores_a, 0.0).astype(jnp.bfloat16)
    back = jnp.where(same_tenant, scores_b, 0.0).astype(jnp.bfloat16)
    over_tokens = (((0,), (0,)), ((), ()))
    grad_a = lax.dot_general(back, token_rows, over_tokens, preferred_element_type=jnp.float32)
    grad_b = lax.dot_general(hidden, grad_rows, over_tokens, preferred_element_type=jnp.float32)
    return (grad_a, grad_b)


def local(
    tokens,
    cotangent,
    factor_a,
    factor_b,
    moment_a,
    moment_b,
    second_a,
    second_b,
    token_counts,
    rank_blocks,
):
    tok_rows = tokens.shape[0]
    own_rows = moment_a.shape[0]
    context_index = lax.axis_index("ctx")
    replica_index = lax.axis_index("dp")
    rank_ends = jnp.cumsum(rank_blocks * 8)
    half_rows = tok_rows // 2
    token_rows = lax.dynamic_slice_in_dim(tokens, replica_index * half_rows, half_rows, 0)
    grad_rows = lax.dynamic_slice_in_dim(cotangent, replica_index * half_rows, half_rows, 0)
    positions = (
        context_index * tok_rows
        + replica_index * half_rows
        + jnp.arange(half_rows, dtype=jnp.int32)
    )
    all_a, all_b = (
        lax.all_gather(factor_a.astype(jnp.bfloat16), "ctx", axis=0, tiled=True),
        lax.all_gather(factor_b.astype(jnp.bfloat16), "ctx", axis=0, tiled=True),
    )
    rank_rows = jnp.arange(all_a.shape[0], dtype=jnp.int32)
    term_a, term_b = partial_grads(
        token_rows, grad_rows, all_a, all_b, positions, rank_rows, token_counts, rank_ends
    )
    grad_a, grad_b = (
        lax.psum_scatter(term_a, ("ctx", "dp"), scatter_dimension=0, tiled=True),
        lax.psum_scatter(term_b, ("ctx", "dp"), scatter_dimension=0, tiled=True),
    )
    owned_a = lax.dynamic_slice_in_dim(factor_a, replica_index * own_rows, own_rows, 0)
    owned_b = lax.dynamic_slice_in_dim(factor_b, replica_index * own_rows, own_rows, 0)
    step_a, new_moment_a, new_second_a = adamw(owned_a, grad_a, moment_a, second_a)
    step_b, new_moment_b, new_second_b = adamw(owned_b, grad_b, moment_b, second_b)
    new_a, new_b = (
        lax.all_gather(step_a, "dp", axis=0, tiled=True),
        lax.all_gather(step_b, "dp", axis=0, tiled=True),
    )
    return (new_a, new_b, new_moment_a, new_second_a, new_moment_b, new_second_b)


def solution(mesh):
    return jax.shard_map(
        local,
        mesh=mesh,
        in_specs=(
            P(("group", "ctx"), None),
            P(("group", "ctx"), None),
            P(("group", "ctx"), None),
            P(("group", "ctx"), None),
            P(("group", "ctx", "dp"), None),
            P(("group", "ctx", "dp"), None),
            P(("group", "ctx", "dp"), None),
            P(("group", "ctx", "dp"), None),
            P("group"),
            P("group"),
        ),
        out_specs=(
            P(("group", "ctx"), None),
            P(("group", "ctx"), None),
            P(("group", "ctx", "dp"), None),
            P(("group", "ctx", "dp"), None),
            P(("group", "ctx", "dp"), None),
            P(("group", "ctx", "dp"), None),
        ),
        check_vma=False,
    )
```

profile of v0, /device:TPU:0, one launch (start us, length us, event | category | flops | bytes accessed | tf_op | source)
XLA Modules:
  0.0 225.6 jit_solution(17440447425052481211)
XLA Ops:
  7.2 0.0 copy-start
  7.2 0.0 all-gather.2.cloned.1.call-start
  7.2 2.0 convert_element_type.22
  9.2 0.0 all-gather.2.cloned.1.call-update
  9.2 0.0 reduce-scatter.5.cloned.1.call-start
  9.3 0.8 reduce-window.16
  10.1 0.7 multiply_bitcast_fusion
  10.8 0.2 reduce-window.17
  11.0 0.1 convert_reduce_fusion.1
  11.1 0.1 convert_reduce_fusion
  11.1 0.0 copy-start.4
  11.1 57.0 %all-gather.2.cloned.1.call-done = bf16[256,5120]{1,0:T(8,128)(2,1)} async-done(((bf16[32,5120]{1,0:T(8,128)(2,1)}), bf16[256,5120]{1,0:T(8,128)(2,1)}) %all-gather.2.cloned.1.call-update) | async-done | bytes 2621456 | tf_op jit(solution)/shard_map/all_gather | solution.py:69
  68.2 0.0 copy-done
  68.2 6.8 %fusion.12 = f32[256,1024]{1,0:T(8,128)} fusion(bf16[256,5120]{1,0:T(8,128)(2,1)} %all-gather.2.cloned.1.call-done, bf16[1024,5120]{1,0:T(8,128)(2,1)} %param.10, s32[]{:T(128)S(6)} %select_n.16, bf16[1024,1024]{1,0:T(8,128)(2,1)S(1)} %copy-done, s32[256]{0:T(256)S(1)} %convert_reduce_fusion.1, s32[512]{0:T(512)S(1)} %convert_reduce_fusion), kind=kOutput, calls=%fused_computation.8 | convolution fusion | flops 1611005952 | bytes 9965568 | tf_op jit(solution)/shard_map/dot_general | solution.py:39
  74.9 0.0 reduce-scatter.5.cloned.1.call-update
  75.0 0.0 reduce-scatter.3.cloned.1.call-start
  75.0 0.0 copy-done.4
  75.0 31.5 %all_gather.12 = bf16[256,1024]{1,0:T(8,128)(2,1)S(1)} all-gather(bf16[32,1024]{1,0:T(8,128)(2,1)S(1)} %convert_element_type.20), channel_id=1, replica_groups=mesh['group'=2,'ctx'=8,'dp'=2] {'ctx'}, dimensions={0}, use_global_device_ids=true | all-gather | bytes 589824 | tf_op jit(solution)/shard_map/all_gather | solution.py:70
  106.6 7.3 %fusion.2 = f32[256,5120]{1,0:T(8,128)} fusion(bf16[1024,5120]{1,0:T(8,128)(2,1)} %param.10, s32[]{:T(128)S(6)} %select_n.16, bf16[256,1024]{1,0:T(8,128)(2,1)S(1)} %all_gather.12, bf16[1024,1024]{1,0:T(8,128)(2,1)S(1)} %copy-done, s32[256]{0:T(256)S(1)} %convert_reduce_fusion.1, s32[512]{0:T(512)S(1)} %convert_reduce_fusion), kind=kOutput, calls=%fused_computation.2 | convolution fusion | flops 1611005952 | bytes 12062720 | tf_op jit(solution)/shard_map/dot_general | solution.py:38
  113.9 0.0 copy-start.1
  113.9 0.0 reduce-scatter.3.cloned.1.call-update
  113.9 17.5 %reduce-scatter.5.cloned.1.call-done = f32[16,1024]{1,0:T(8,128)} async-done(((f32[256,1024]{1,0:T(8,128)}), f32[16,1024]{1,0:T(8,128)}) %reduce-scatter.5.cloned.1.call-update) | async-done | bytes 65552 | tf_op jit(solution)/shard_map/reduce_scatter | solution.py:78
  131.4 1.6 multiply_subtract_fusion.1
  133.0 1.9 all_gather.15
  134.9 78.4 %reduce-scatter.3.cloned.1.call-done = f32[16,5120]{1,0:T(8,128)} async-done(((f32[256,5120]{1,0:T(8,128)}), f32[16,5120]{1,0:T(8,128)}) %reduce-scatter.3.cloned.1.call-update) | async-done | bytes 327696 | tf_op jit(solution)/shard_map/reduce_scatter | solution.py:77
  213.3 0.0 copy-done.1
  213.3 0.0 copy-done.2
  213.3 0.0 copy-done.3
  213.3 2.0 multiply_subtract_fusion
  215.3 2.3 %all_gather.13 = f32[32,5120]{1,0:T(8,128)S(1)} all-gather(f32[16,5120]{1,0:T(8,128)S(1)} %get-tuple-element.9), channel_id=1, replica_groups=mesh['group'=2,'ctx'=8,'dp'=2] {'dp'}, dimensions={0}, use_global_device_ids=true | all-gather | bytes 983040 | tf_op jit(solution)/shard_map/all_gather | solution.py:85
  217.6 0.8 copy.18
  218.4 0.7 copy.19
  (4 shorter events, 0.0 us)
Async XLA Ops:
  7.2 61.0 %copy-start = (bf16[1024,1024]{1,0:T(8,128)(2,1)S(1)}, bf16[1024,1024]{1,0:T(8,128)(2,1)}, u32[]{:S(2)}) copy-start(bf16[1024,1024]{1,0:T(8,128)(2,1)} %param.11) | copy-start | bytes 6291460
  7.2 61.0 %all-gather.2.cloned.1.call-start = ((), (), s32[]{:S(2)}) async-start(), calls=%async_computation.3 | async-start | bytes 2949120 | tf_op jit(solution)/shard_map/all_gather | solution.py:69
  9.2 122.1 %reduce-scatter.5.cloned.1.call-start = ((), (), s32[]{:S(2)}) async-start(), calls=%async_computation.4 | async-start | bytes 1114112 | tf_op jit(solution)/shard_map/reduce_scatter | solution.py:78
  11.1 63.9 %copy-start.4 = (f32[32,1024]{1,0:T(8,128)S(1)}, f32[32,1024]{1,0:T(8,128)}, u32[]{:S(2)}) copy-start(f32[32,1024]{1,0:T(8,128)} %param.13) | copy-start | bytes 393220
  75.0 138.3 %reduce-scatter.3.cloned.1.call-start = ((), (), s32[]{:S(2)}) async-start(), calls=%async_computation.2 | async-start | bytes 5570560 | tf_op jit(solution)/shard_map/reduce_scatter | solution.py:77
  113.9 99.4 %copy-start.1 = (f32[32,5120]{1,0:T(8,128)S(1)}, f32[32,5120]{1,0:T(8,128)}, u32[]{:S(2)}) copy-start(f32[32,5120]{1,0:T(8,128)} %param.12) | copy-start | bytes 1966084
  113.9 99.4 %copy-start.2 = (f32[16,5120]{1,0:T(8,128)S(1)}, f32[16,5120]{1,0:T(8,128)}, u32[]{:S(2)}) copy-start(f32[16,5120]{1,0:T(8,128)} %param.14) | copy-start | bytes 983044
  113.9 99.4 %copy-start.3 = (f32[16,5120]{1,0:T(8,128)S(1)}, f32[16,5120]{1,0:T(8,128)}, u32[]{:S(2)}) copy-start(f32[16,5120]{1,0:T(8,128)} %param.16) | copy-start | bytes 983044
Sparse Core Ops, SparseCore 0:
  10.8 57.3 all-gather.1
  75.1 56.2 reduce-scatter.4
  135.8 77.4 reduce-scatter.2
where the time goes:
time: 226 us
  waiting for transfers between devices  153 us (68%)
  blocking collectives  35.7 us (16%)
  matrix products  14.1 us (6%)
  between operations  13.8 us (6%)
  other arithmetic  7.48 us (3%)
    reduce_scatter x1, waiting for transfers between devices, local(): lax.psum_scatter(term_a, ('ctx', 'dp'), scatter_dimension=0, tiled=True)  78.4 us
    all_gather x1, waiting for transfers between devices, local(): lax.all_gather(factor_a.astype(jnp.bfloat16), 'ctx', axis=0, tiled=True)  57 us
    all_gather x1, blocking collectives, local(): lax.all_gather(factor_b.astype(jnp.bfloat16), 'ctx', axis=0, tiled=True)  31.5 us
    reduce_scatter x1, waiting for transfers between devices, local(): lax.psum_scatter(term_b, ('ctx', 'dp'), scatter_dimension=0, tiled=True)  17.5 us
    dot_general x1, matrix products, partial_grads(): lax.dot_general(back, token_rows, over_tokens, preferred_element_type=jnp...  7.32 us
    dot_general x1, matrix products, partial_grads(): lax.dot_general(hidden, grad_rows, over_tokens, preferred_element_type=jn...  6.78 us
  transfers between devices with their start and end apart: 3, of which 3 were waited for; matrix products, arithmetic and copies ran while one was open for 5% of the time, Pallas kernels for 0%

commit v1 on v0

--- a/solution.py
+++ b/solution.py
@@ -1,6 +1,10 @@
+import functools
+
 import jax
 import jax.numpy as jnp
 from jax import lax
+from jax.experimental import pallas as pl
+from jax.experimental.pallas import tpu as pltpu
 from jax.sharding import PartitionSpec as P
 
 beta_one = 0.9
@@ -40,7 +44,7 @@
     return (grad_a, grad_b)
 
 
-def local(
+def local_plain(
     tokens,
     cotangent,
     factor_a,
@@ -88,7 +92,343 @@
     return (new_a, new_b, new_moment_a, new_second_a, new_moment_b, new_second_b)
 
 
+MESH = pl.DeviceIdType.MESH
+HBM = pl.BlockSpec(memory_space=pl.ANY)
+SMEM = pl.BlockSpec(memory_space=pltpu.SMEM)
+
+
+def ring_kernel(
+    n,
+    chunks,
+    tokens,
+    cotangent,
+    factor_a,
+    factor_b,
+    moment_a,
+    moment_b,
+    second_a,
+    second_b,
+    token_counts,
+    rank_blocks,
+    out_a,
+    out_b,
+    out_moment_a,
+    out_second_a,
+    out_moment_b,
+    out_second_b,
+    tok,
+    cot,
+    param,
+    moment,
+    second,
+    low_a,
+    low_b,
+    back,
+    hidden,
+    scores,
+    grads,
+    whole_in,
+    half_in,
+    load_sem,
+    store_sem,
+    gather_send,
+    gather_recv,
+    reduce_send,
+    reduce_recv,
+    pair_send,
+    pair_recv,
+):
+    hops = n // 2
+    width_a = factor_a.shape[1]
+    width_b = factor_b.shape[1]
+    own = moment_a.shape[0]
+    toks = tokens.shape[0]
+    rows = n * own
+    group = lax.axis_index("group")
+    ctx = lax.axis_index("ctx")
+    core = lax.axis_index("dp")
+    column, odd = ctx // 2, ctx % 2
+    place = column + odd * (n - 1 - 2 * column)
+
+    def index_at(position):
+        q = (position + 2 * n) % n
+        return 2 * q + (q // hops) * (2 * n - 1 - 4 * q)
+
+    def block(position):
+        return pl.ds(pl.multiple_of(index_at(position) * own, own), own)
+
+    signs = (1, -1)
+    neighbours = [(group, index_at(place + s), core) for s in signs]
+    partner = (group, ctx, 1 - core)
+    my_half = pl.ds(pl.multiple_of(core * own, own), own)
+    cols_a, cols_b = pl.ds(0, width_a), pl.ds(width_a, width_b)
+
+    loads = [
+        pltpu.make_async_copy(source, target, load_sem.at[i])
+        for i, (source, target) in enumerate(
+            (
+                (factor_b.at[my_half], param.at[:, cols_b]),
+                (factor_a.at[my_half], param.at[:, cols_a]),
+                (cotangent, cot),
+                (tokens, tok),
+                (moment_a, moment.at[:, cols_a]),
+                (moment_b, moment.at[:, cols_b]),
+                (second_a, second.at[:, cols_a]),
+                (second_b, second.at[:, cols_b]),
+            )
+        )
+    ]
+    for load in loads:
+        load.start()
+    barrier = pltpu.get_barrier_semaphore()
+    for device in (*neighbours, partner):
+        pl.semaphore_signal(barrier, inc=1, device_id=device, device_id_type=MESH)
+    mine = block(place)
+    loads[0].wait()
+    low_b[mine, :] = param[:, width_a:].astype(jnp.bfloat16)
+    loads[1].wait()
+    low_a[mine, :] = param[:, :width_a].astype(jnp.bfloat16)
+    pl.semaphore_wait(barrier, 3)
+
+    sent = []
+
+    def gather_copy(which, d, t):
+        low, width = ((low_a, width_a), (low_b, width_b))[which]
+        where = block(place - signs[d] * (t - 1))
+        cols = pl.ds(d * (width // 2), width // 2) if t == hops else pl.ds(0, width)
+        return pltpu.make_async_remote_copy(
+            src_ref=low.at[where, cols],
+            dst_ref=low.at[where, cols],
+            send_sem=gather_send.at[which, d, t - 1],
+            recv_sem=gather_recv.at[which, d, t - 1],
+            device_id=neighbours[d],
+            device_id_type=MESH,
+        )
+
+    def gather(which, t):
+        for d in range(2):
+            if t > 1:
+                arrived[which, d].wait_recv()
+            if t <= hops:
+                copy = gather_copy(which, d, t)
+                copy.start()
+                arrived[which, d] = copy
+                sent.append(copy)
+
+    arrived = {}
+    gather(1, 1)
+    gather(0, 1)
+    for t in range(2, hops + 1):
+        gather(1, t)
+    gather(0, 2)
+
+    def tenant(position, counts, scale):
+        total = jnp.zeros_like(position)
+        end = 0
+        for t in range(counts.shape[0]):
+            end = end + counts[t] * scale
+            total = total + (position >= end).astype(jnp.int32)
+        return total
+
+    row = lax.broadcasted_iota(jnp.int32, (rows, 1), 0)
+    row = (row // own) * (2 * own) + core * own + row % own
+    token = ctx * toks + lax.broadcasted_iota(jnp.int32, (1, toks), 1)
+    same = tenant(row, rank_blocks, 8) == tenant(token, token_counts, 1)
+    last = (((1,), (1,)), ((), ()))
+
+    gather(1, hops + 1)
+    loads[2].wait()
+    scores_b = lax.dot_general(low_b[...], cot[...], last, preferred_element_type=jnp.float32)
+    back[...] = jnp.where(same, scores_b, 0.0).astype(jnp.bfloat16)
+    for t in range(3, hops):
+        gather(0, t)
+
+    reducing = {}
+
+    def reduce_step(c, t):
+        start, width = chunks[c]
+        half = width // 2
+        for d in range(2):
+            if t > 1:
+                reducing[c, d].wait_recv()
+            if t > hops:
+                continue
+            where = block(place + signs[d] * (hops + 1 - t))
+            if t == 1:
+                source = grads.at[where, pl.ds(start + d * half, half)]
+                target = half_in.at[d, :, pl.ds(start // 2, half)]
+            else:
+                if t == 2:
+                    cols = pl.ds(start + d * half, half)
+                    grads[where, cols] += half_in[d, :, start // 2 : start // 2 + half]
+                else:
+                    cols = pl.ds(start, width)
+                    grads[where, cols] += whole_in[d, t - 3, :, start : start + width]
+                source = grads.at[where, pl.ds(start, width)]
+                target = whole_in.at[d, t - 2, :, pl.ds(start, width)]
+            copy = pltpu.make_async_remote_copy(
+                src_ref=source,
+                dst_ref=target,
+                send_sem=reduce_send.at[c, d, t - 1],
+                recv_sem=reduce_recv.at[c, d, t - 1],
+                device_id=neighbours[d],
+                device_id_type=MESH,
+            )
+            copy.start()
+            reducing[c, d] = copy
+            sent.append(copy)
+
+    loads[3].wait()
+    last_c = len(chunks) - 1
+    tile = 512
+
+    def grad_tile(start):
+        def body(i, carry):
+            cols = pl.ds(pl.multiple_of(start + i * tile, tile), tile)
+            grads[:, cols] = jnp.dot(
+                back[...], tok[:, cols], preferred_element_type=jnp.float32
+            )
+            return carry
+
+        return body
+
+    for c in range(last_c):
+        lax.fori_loop(0, chunks[c][1] // tile, grad_tile(chunks[c][0]), 0)
+        reduce_step(c, 1)
+        if c == 0:
+            gather(0, hops)
+    for c in range(last_c):
+        reduce_step(c, 2)
+    gather(0, hops + 1)
+
+    depth = 1024
+    scores[...] = jnp.zeros_like(scores)
+
+    def score_tile(i, carry):
+        cols = pl.ds(pl.multiple_of(i * depth, depth), depth)
+        scores[...] += lax.dot_general(
+            low_a[:, cols], tok[:, cols], last, preferred_element_type=jnp.float32
+        )
+        return carry
+
+    lax.fori_loop(0, width_a // depth, score_tile, 0)
+    hidden[...] = jnp.where(same, scores[...], 0.0).astype(jnp.bfloat16)
+    grads[:, cols_b] = jnp.dot(hidden[...], cot[...], preferred_element_type=jnp.float32)
+    reduce_step(last_c, 1)
+    for t in range(3, hops + 1):
+        for c in range(last_c):
+            reduce_step(c, t)
+        reduce_step(last_c, t - 1)
+
+    for load in loads[4:]:
+        load.wait()
+    stores = []
+
+    def finish(c):
+        start, width = chunks[c]
+        cols = pl.ds(start, width)
+        reduce_step(c, hops + 1)
+        grad = grads[mine, cols] + whole_in[0, hops - 2, :, start : start + width]
+        grad = grad + whole_in[1, hops - 2, :, start : start + width]
+        new = adamw(param[:, cols], grad, moment[:, cols], second[:, cols])
+        param[:, cols], moment[:, cols], second[:, cols] = new
+        if start < width_a:
+            outs, at = (out_a, out_moment_a, out_second_a), pl.ds(start, width)
+        else:
+            outs, at = (out_b, out_moment_b, out_second_b), pl.ds(start - width_a, width)
+        copy = pltpu.make_async_remote_copy(
+            src_ref=param.at[:, cols],
+            dst_ref=outs[0].at[my_half, at],
+            send_sem=pair_send.at[c],
+            recv_sem=pair_recv.at[c],
+            device_id=partner,
+            device_id_type=MESH,
+        )
+        copy.start()
+        sent.append(copy)
+        targets = (outs[0].at[my_half, at], outs[1].at[:, at], outs[2].at[:, at])
+        for i, (source, target) in enumerate(zip((param, moment, second), targets)):
+            store = pltpu.make_async_copy(source.at[:, cols], target, store_sem.at[c, i])
+            store.start()
+            stores.append(store)
+        return copy
+
+    pairs = []
+    for c in range(last_c):
+        pairs.append(finish(c))
+        if c == 0:
+            reduce_step(last_c, hops)
+    pairs.append(finish(last_c))
+    for pair in pairs:
+        pair.wait_recv()
+    for store in stores:
+        store.wait()
+    for copy in sent:
+        copy.wait_send()
+
+
+def local_ring(n, *args):
+    tokens, cotangent, factor_a, factor_b, moment_a = args[:5]
+    toks, width_a = tokens.shape
+    width_b = cotangent.shape[1]
+    own = moment_a.shape[0]
+    width = width_a + width_b
+    rows = n * own
+    hops = n // 2
+    half = width_a // 2
+    chunks = ((0, half), (half, half), (width_a, width_b))
+    f32, bf16 = jnp.float32, jnp.bfloat16
+    count = len(chunks)
+    dma = pltpu.SemaphoreType.DMA
+    like = jax.ShapeDtypeStruct
+    return pl.pallas_call(
+        functools.partial(ring_kernel, n, chunks),
+        out_shape=(
+            like(factor_a.shape, f32),
+            like(factor_b.shape, f32),
+            like((own, width_a), f32),
+            like((own, width_a), f32),
+            like((own, width_b), f32),
+            like((own, width_b), f32),
+        ),
+        in_specs=[HBM] * 8 + [SMEM] * 2,
+        out_specs=(HBM,) * 6,
+        scratch_shapes=[
+            pltpu.VMEM((toks, width_a), bf16),
+            pltpu.VMEM((toks, width_b), bf16),
+            pltpu.VMEM((own, width), f32),
+            pltpu.VMEM((own, width), f32),
+            pltpu.VMEM((own, width), f32),
+            pltpu.VMEM((rows, width_a), bf16),
+            pltpu.VMEM((rows, width_b), bf16),
+            pltpu.VMEM((rows, toks), bf16),
+            pltpu.VMEM((rows, toks), bf16),
+            pltpu.VMEM((rows, toks), f32),
+            pltpu.VMEM((rows, width), f32),
+            pltpu.VMEM((2, hops - 1, own, width), f32),
+            pltpu.VMEM((2, own, width // 2), f32),
+            dma((8,)),
+            dma((count, 3)),
+            dma((2, 2, hops)),
+            dma((2, 2, hops)),
+            dma((count, 2, hops)),
+            dma((count, 2, hops)),
+            dma((count,)),
+            dma((count,)),
+        ],
+        compiler_params=pltpu.CompilerParams(
+            collective_id=0, has_side_effects=True, vmem_limit_bytes=50 << 20
+        ),
+    )(*args)
+
+
 def solution(mesh):
+    n = mesh.shape["ctx"]
+    if n >= 4 and n % 2 == 0 and 256 % (32 * n) == 0:
+        local = functools.partial(local_ring, n)
+    else:
+        local = local_plain
+
     return jax.shard_map(
         local,
         mesh=mesh,

time: 226 us -> 71.4 us (0.32)
  waiting for transfers between devices: 153 us -> 0 us
  Pallas kernels: 0 us -> 59.2 us
  blocking collectives: 35.7 us -> 0 us
  matrix products: 14.1 us -> 0 us
  between operations: 13.8 us -> 0.66 us
  local copies, waits for them, and re-layouts: 1.52 us -> 11.1 us
  other arithmetic: 7.48 us -> 0 us
    reduce_scatter x2 -> x0, waiting for transfers between devices: 95.9 us -> none  [the longest x1 78.4 us: local(): lax.psum_scatter(term_a, ('ctx', 'dp'), scatter_dimension=0, tiled=True)]
    pallas_call x0 -> x1, Pallas kernels: none -> 59.2 us  [local_ring(): pl.pallas_call(functools.partial(ring_kernel, n, chunks), out_shape=(like...]
    all_gather x1 -> x0, waiting for transfers between devices: 57 us -> none  [local(): lax.all_gather(factor_a.astype(jnp.bfloat16), 'ctx', axis=0, tiled=True)]
    all_gather x3 -> x0, blocking collectives: 35.7 us -> none  [the longest x1 31.5 us: local(): lax.all_gather(factor_b.astype(jnp.bfloat16), 'ctx', axis=0, tiled=True)]
    dot_general x2 -> x0, matrix products: 14.1 us -> none  [the longest x1 7.32 us: partial_grads(): lax.dot_general(back, token_rows, over_tokens, preferred_element_type=jnp...]
    unnamed x12 -> x22, local copies, waits for them, and re-layouts: 1.52 us -> 11.1 us
    sub x2 -> x0, other arithmetic: 3.64 us -> none  [adamw(): param - learn_rate * (update + decay_rate * param)]
  transfers between devices with their start and end apart: 3 -> 0, of which waited for: 3 -> 0; matrix products, arithmetic and copies ran while one was open for 5% -> 0% of each run, Pallas kernels for 0% -> 0%
where the time goes in v1:
time: 71.4 us; the launch traced here: 71 us
  Pallas kernels  59.2 us (83%)
  local copies, waits for them, and re-layouts  11.1 us (16%)
    pallas_call x1, Pallas kernels, local_ring(): pl.pallas_call(functools.partial(ring_kernel, n, chunks), out_shape=(like...  59.2 us
    unnamed x22, local copies, waits for them, and re-layouts  11.1 us

profile of v1, /device:TPU:0, one launch (start us, length us, event | category | flops | bytes accessed | tf_op | source)
XLA Modules:
  0.0 71.0 jit_solution(13164759225030898197)
XLA Ops:
  0.6 0.0 copy-start
  0.6 1.1 %copy-done = f32[32,5120]{1,0:T(8,128)S(1)} copy-done((f32[32,5120]{1,0:T(8,128)S(1)}, f32[32,5120]{1,0:T(8,128)}, u32[]{:S(2)}) %copy-start) | copy-done | bytes 655384
  1.7 0.0 copy-start.1
  1.7 1.0 %copy-done.1 = f32[16,5120]{1,0:T(8,128)S(1)} copy-done((f32[16,5120]{1,0:T(8,128)S(1)}, f32[16,5120]{1,0:T(8,128)}, u32[]{:S(2)}) %copy-start.1) | copy-done | bytes 327704
  2.7 0.0 copy-start.2
  2.7 1.0 %copy-done.2 = f32[16,5120]{1,0:T(8,128)S(1)} copy-done((f32[16,5120]{1,0:T(8,128)S(1)}, f32[16,5120]{1,0:T(8,128)}, u32[]{:S(2)}) %copy-start.2) | copy-done | bytes 327704
  3.7 0.0 copy-start.3
  3.7 0.9 %copy-done.3 = f32[32,1024]{1,0:T(8,128)S(1)} copy-done((f32[32,1024]{1,0:T(8,128)S(1)}, f32[32,1024]{1,0:T(8,128)}, u32[]{:S(2)}) %copy-start.3) | copy-done | bytes 131096
  4.6 0.0 copy-start.4
  4.6 0.8 %copy-done.4 = f32[16,1024]{1,0:T(8,128)S(1)} copy-done((f32[16,1024]{1,0:T(8,128)S(1)}, f32[16,1024]{1,0:T(8,128)}, u32[]{:S(2)}) %copy-start.4) | copy-done | bytes 65560
  5.4 0.0 copy-start.5
  5.4 0.8 %copy-done.5 = f32[16,1024]{1,0:T(8,128)S(1)} copy-done((f32[16,1024]{1,0:T(8,128)S(1)}, f32[16,1024]{1,0:T(8,128)}, u32[]{:S(2)}) %copy-start.5) | copy-done | bytes 65560
  6.3 0.0 copy-start.6
  6.3 0.7 copy-done.6
  6.9 0.0 copy-start.7
  6.9 0.7 copy-done.7
  7.6 59.2 %shard_map.145 = (f32[32,5120]{1,0:T(8,128)S(1)}, f32[32,1024]{1,0:T(8,128)S(1)}, f32[16,5120]{1,0:T(8,128)S(1)}, f32[16,5120]{1,0:T(8,128)S(1)}, f32[16,1024]{1,0:T(8,128)S(1)}, /*index=5*/f32[16,1024]{1,0:T(8,128)S(1)}) custom-call(bf16[1024,5120]{1,0:T(8,128)(2,1)} %tokens.1, bf16[1024,1024]{1,0:T(8,128)(2,1)} %cotangent.1, f32[32,5120]{1,0:T(8,128)S(1)} %copy-done, ...), custom_call_target="tpu_custom_call" | custom-call | tf_op jit(solution)/shard_map/pallas_call | solution.py:384
  66.8 0.8 %copy.22 = f32[32,5120]{1,0:T(8,128)} copy(f32[32,5120]{1,0:T(8,128)S(1)} %get-tuple-element.12) | data formatting | bytes 1310720
  67.6 0.7 copy.23
  68.3 0.7 %copy.24 = f32[16,5120]{1,0:T(8,128)} copy(f32[16,5120]{1,0:T(8,128)S(1)} %get-tuple-element.14) | data formatting | bytes 655360
  69.0 0.7 %copy.25 = f32[16,5120]{1,0:T(8,128)} copy(f32[16,5120]{1,0:T(8,128)S(1)} %get-tuple-element.15) | data formatting | bytes 655360
  69.7 0.6 copy.26
  70.4 0.6 copy.27
Async XLA Ops:
  0.6 1.1 %copy-start = (f32[32,5120]{1,0:T(8,128)S(1)}, f32[32,5120]{1,0:T(8,128)}, u32[]{:S(2)}) copy-start(f32[32,5120]{1,0:T(8,128)} %factor_a.1) | copy-start | bytes 1966084
  1.7 1.0 %copy-start.1 = (f32[16,5120]{1,0:T(8,128)S(1)}, f32[16,5120]{1,0:T(8,128)}, u32[]{:S(2)}) copy-start(f32[16,5120]{1,0:T(8,128)} %moment_a.1) | copy-start | bytes 983044
  2.7 1.0 %copy-start.2 = (f32[16,5120]{1,0:T(8,128)S(1)}, f32[16,5120]{1,0:T(8,128)}, u32[]{:S(2)}) copy-start(f32[16,5120]{1,0:T(8,128)} %second_a.1) | copy-start | bytes 983044
  3.7 0.9 %copy-start.3 = (f32[32,1024]{1,0:T(8,128)S(1)}, f32[32,1024]{1,0:T(8,128)}, u32[]{:S(2)}) copy-start(f32[32,1024]{1,0:T(8,128)} %factor_b.1) | copy-start | bytes 393220
  4.6 0.8 %copy-start.4 = (f32[16,1024]{1,0:T(8,128)S(1)}, f32[16,1024]{1,0:T(8,128)}, u32[]{:S(2)}) copy-start(f32[16,1024]{1,0:T(8,128)} %moment_b.1) | copy-start | bytes 196612
  5.4 0.8 %copy-start.5 = (f32[16,1024]{1,0:T(8,128)S(1)}, f32[16,1024]{1,0:T(8,128)}, u32[]{:S(2)}) copy-start(f32[16,1024]{1,0:T(8,128)} %second_b.1) | copy-start | bytes 196612
  6.3 0.7 copy-start.6
  6.9 0.7 copy-start.7

commit v2 on v1

--- a/solution.py
+++ b/solution.py
@@ -93,8 +93,8 @@
 
 
 MESH = pl.DeviceIdType.MESH
-HBM = pl.BlockSpec(memory_space=pl.ANY)
-SMEM = pl.BlockSpec(memory_space=pltpu.SMEM)
+ANY = pl.BlockSpec(memory_space=pl.ANY)
+HBM = pl.BlockSpec(memory_space=pltpu.HBM)
 
 
 def ring_kernel(
@@ -129,6 +129,8 @@
     grads,
     whole_in,
     half_in,
+    counts,
+    blocks,
     load_sem,
     store_sem,
     gather_send,
@@ -175,6 +177,8 @@
                 (moment_b, moment.at[:, cols_b]),
                 (second_a, second.at[:, cols_a]),
                 (second_b, second.at[:, cols_b]),
+                (token_counts, counts),
+                (rank_blocks, blocks),
             )
         )
     ]
@@ -192,35 +196,41 @@
 
     sent = []
 
-    def gather_copy(which, d, t):
-        low, width = ((low_a, width_a), (low_b, width_b))[which]
-        where = block(place - signs[d] * (t - 1))
-        cols = pl.ds(d * (width // 2), width // 2) if t == hops else pl.ds(0, width)
-        return pltpu.make_async_remote_copy(
-            src_ref=low.at[where, cols],
-            dst_ref=low.at[where, cols],
-            send_sem=gather_send.at[which, d, t - 1],
-            recv_sem=gather_recv.at[which, d, t - 1],
-            device_id=neighbours[d],
-            device_id_type=MESH,
-        )
+    quarter = width_a // 2
+    pieces = ((low_a, 0, quarter), (low_a, quarter, quarter), (low_b, 0, width_b))
+    gathering = {}
 
     def gather(which, t):
+        low, start, width = pieces[which]
+        half = width // 2
         for d in range(2):
             if t > 1:
-                arrived[which, d].wait_recv()
-            if t <= hops:
-                copy = gather_copy(which, d, t)
-                copy.start()
-                arrived[which, d] = copy
-                sent.append(copy)
-
-    arrived = {}
+                gathering[which, d].wait_recv()
+            if t > hops:
+                continue
+            where = block(place - signs[d] * (t - 1))
+            cols = pl.ds(start + d * half, half) if t == hops else pl.ds(start, width)
+            copy = pltpu.make_async_remote_copy(
+                src_ref=low.at[where, cols],
+                dst_ref=low.at[where, cols],
+                send_sem=gather_send.at[which, d, t - 1],
+                recv_sem=gather_recv.at[which, d, t - 1],
+                device_id=neighbours[d],
+                device_id_type=MESH,
+            )
+            copy.start()
+            gathering[which, d] = copy
+            sent.append(copy)
+
+    gather(2, 1)
+    gather(0, 1)
+    gather(2, 2)
     gather(1, 1)
-    gather(0, 1)
-    for t in range(2, hops + 1):
+    for t in range(3, hops + 1):
+        gather(2, t)
+        gather(0, t - 1)
+    for t in range(2, hops - 1):
         gather(1, t)
-    gather(0, 2)
 
     def tenant(position, counts, scale):
         total = jnp.zeros_like(position)
@@ -233,15 +243,16 @@
     row = lax.broadcasted_iota(jnp.int32, (rows, 1), 0)
     row = (row // own) * (2 * own) + core * own + row % own
     token = ctx * toks + lax.broadcasted_iota(jnp.int32, (1, toks), 1)
-    same = tenant(row, rank_blocks, 8) == tenant(token, token_counts, 1)
+    loads[8].wait()
+    loads[9].wait()
+    same = tenant(row, blocks, 8) == tenant(token, counts, 1)
     last = (((1,), (1,)), ((), ()))
 
-    gather(1, hops + 1)
+    gather(2, hops + 1)
     loads[2].wait()
     scores_b = lax.dot_general(low_b[...], cot[...], last, preferred_element_type=jnp.float32)
     back[...] = jnp.where(same, scores_b, 0.0).astype(jnp.bfloat16)
-    for t in range(3, hops):
-        gather(0, t)
+    gather(1, hops - 1)
 
     reducing = {}
 
@@ -280,26 +291,18 @@
 
     loads[3].wait()
     last_c = len(chunks) - 1
-    tile = 512
-
-    def grad_tile(start):
-        def body(i, carry):
-            cols = pl.ds(pl.multiple_of(start + i * tile, tile), tile)
-            grads[:, cols] = jnp.dot(
-                back[...], tok[:, cols], preferred_element_type=jnp.float32
-            )
-            return carry
-
-        return body
-
     for c in range(last_c):
-        lax.fori_loop(0, chunks[c][1] // tile, grad_tile(chunks[c][0]), 0)
+        start, width = chunks[c]
+        grads[:, start : start + width] = jnp.dot(
+            back[...], tok[:, start : start + width], preferred_element_type=jnp.float32
+        )
         reduce_step(c, 1)
-        if c == 0:
-            gather(0, hops)
+        if c < 2:
+            gather(c, hops)
     for c in range(last_c):
         reduce_step(c, 2)
     gather(0, hops + 1)
+    gather(1, hops + 1)
 
     depth = 1024
     scores[...] = jnp.zeros_like(scores)
@@ -315,12 +318,17 @@
     hidden[...] = jnp.where(same, scores[...], 0.0).astype(jnp.bfloat16)
     grads[:, cols_b] = jnp.dot(hidden[...], cot[...], preferred_element_type=jnp.float32)
     reduce_step(last_c, 1)
+    middle = last_c // 2
+    reduce_step(0, 3)
+    reduce_step(last_c, 2)
     for t in range(3, hops + 1):
         for c in range(last_c):
-            reduce_step(c, t)
-        reduce_step(last_c, t - 1)
-
-    for load in loads[4:]:
+            if (c, t) != (0, 3):
+                reduce_step(c, t)
+            if c == middle:
+                reduce_step(last_c, t)
+
+    for load in loads[4:8]:
         load.wait()
     stores = []
 
@@ -353,18 +361,23 @@
             stores.append(store)
         return copy
 
-    pairs = []
-    for c in range(last_c):
-        pairs.append(finish(c))
-        if c == 0:
-            reduce_step(last_c, hops)
-    pairs.append(finish(last_c))
+    pairs = [finish(c) for c in (0, last_c, *range(1, last_c))]
     for pair in pairs:
         pair.wait_recv()
     for store in stores:
         store.wait()
     for copy in sent:
         copy.wait_send()
+
+
+def hand_out(*refs):
+    copies = [
+        pltpu.make_async_copy(refs[i], refs[6 + i], refs[12].at[i]) for i in range(6)
+    ]
+    for copy in copies:
+        copy.start()
+    for copy in copies:
+        copy.wait()
 
 
 def local_ring(n, *args):
@@ -375,13 +388,13 @@
     width = width_a + width_b
     rows = n * own
     hops = n // 2
-    half = width_a // 2
-    chunks = ((0, half), (half, half), (width_a, width_b))
+    part = width_a // 4
+    chunks = (*((i * part, part) for i in range(4)), (width_a, width_b))
     f32, bf16 = jnp.float32, jnp.bfloat16
     count = len(chunks)
     dma = pltpu.SemaphoreType.DMA
     like = jax.ShapeDtypeStruct
-    return pl.pallas_call(
+    results = pl.pallas_call(
         functools.partial(ring_kernel, n, chunks),
         out_shape=(
             like(factor_a.shape, f32),
@@ -391,8 +404,8 @@
             like((own, width_b), f32),
             like((own, width_b), f32),
         ),
-        in_specs=[HBM] * 8 + [SMEM] * 2,
-        out_specs=(HBM,) * 6,
+        in_specs=[HBM] * 10,
+        out_specs=(ANY,) * 6,
         scratch_shapes=[
             pltpu.VMEM((toks, width_a), bf16),
             pltpu.VMEM((toks, width_b), bf16),
@@ -407,19 +420,28 @@
             pltpu.VMEM((rows, width), f32),
             pltpu.VMEM((2, hops - 1, own, width), f32),
             pltpu.VMEM((2, own, width // 2), f32),
-            dma((8,)),
+            pltpu.SMEM(args[8].shape, jnp.int32),
+            pltpu.SMEM(args[9].shape, jnp.int32),
+            dma((10,)),
             dma((count, 3)),
-            dma((2, 2, hops)),
-            dma((2, 2, hops)),
+            dma((3, 2, hops)),
+            dma((3, 2, hops)),
             dma((count, 2, hops)),
             dma((count, 2, hops)),
             dma((count,)),
             dma((count,)),
         ],
         compiler_params=pltpu.CompilerParams(
-            collective_id=0, has_side_effects=True, vmem_limit_bytes=50 << 20
+            collective_id=0, has_side_effects=True, vmem_limit_bytes=63 << 20
         ),
     )(*args)
+    return pl.pallas_call(
+        hand_out,
+        out_shape=tuple(like(r.shape, r.dtype) for r in results),
+        in_specs=[ANY] * 6,
+        out_specs=(HBM,) * 6,
+        scratch_shapes=[dma((6,))],
+    )(*results)
 
 
 def solution(mesh):

time: 71.4 us -> 105 us (1.47)
  Pallas kernels: 59.2 us -> 104 us
  local copies, waits for them, and re-layouts: 11.1 us -> 0 us
    pallas_call x0 -> x1, Pallas kernels: none -> 48.8 us  [local_ring(): pl.pallas_call(hand_out, out_shape=tuple((like(r.shape, r.dtype) for r in...]
    unnamed x22 -> x0, local copies, waits for them, and re-layouts: 11.1 us -> none
    pallas_call x1, Pallas kernels: 59.2 us -> 55.3 us  [local_ring(): pl.pallas_call(functools.partial(ring_kernel, n, chunks), out_shape=(like...]
where the time goes in v2:
time: 105 us
  Pallas kernels  104 us (99%)
    pallas_call x1, Pallas kernels, local_ring(): pl.pallas_call(functools.partial(ring_kernel, n, chunks), out_shape=(like...  55.3 us
    pallas_call x1, Pallas kernels, local_ring(): pl.pallas_call(hand_out, out_shape=tuple((like(r.shape, r.dtype) for r in...  48.8 us

profile of v2, /device:TPU:0, one launch (start us, length us, event | category | flops | bytes accessed | tf_op | source)
XLA Modules:
  0.0 104.8 jit_solution(8381313240349903691)
XLA Ops:
  0.6 55.3 %shard_map.145 = (f32[32,5120]{1,0:T(8,128)}, f32[32,1024]{1,0:T(8,128)}, f32[16,5120]{1,0:T(8,128)}, f32[16,5120]{1,0:T(8,128)}, f32[16,1024]{1,0:T(8,128)}, /*index=5*/f32[16,1024]{1,0:T(8,128)}) custom-call(bf16[1024,5120]{1,0:T(8,128)(2,1)} %tokens.1, bf16[1024,1024]{1,0:T(8,128)(2,1)} %cotangent.1, f32[32,5120]{1,0:T(8,128)} %factor_a.1, ...), custom_call_target="tpu_custom_call" | custom-call | tf_op jit(solution)/shard_map/pallas_call | solution.py:397
  56.0 48.8 %shard_map.146 = (f32[32,5120]{1,0:T(8,128)}, f32[32,1024]{1,0:T(8,128)}, f32[16,5120]{1,0:T(8,128)}, f32[16,5120]{1,0:T(8,128)}, f32[16,1024]{1,0:T(8,128)}, /*index=5*/f32[16,1024]{1,0:T(8,128)}) custom-call(f32[32,5120]{1,0:T(8,128)} %get-tuple-element.12.refs_0_, f32[32,1024]{1,0:T(8,128)} %get-tuple-element.13.refs_1_, ...), custom_call_target="tpu_custom_call" | custom-call | tf_op jit(solution)/shard_map/pallas_call | solution.py:438

commit v3 on v2

--- a/solution.py
+++ b/solution.py
@@ -94,6 +94,7 @@
 
 MESH = pl.DeviceIdType.MESH
 ANY = pl.BlockSpec(memory_space=pl.ANY)
+VMEM = pl.BlockSpec(memory_space=pltpu.VMEM)
 HBM = pl.BlockSpec(memory_space=pltpu.HBM)
 
 
@@ -132,7 +133,6 @@
     counts,
     blocks,
     load_sem,
-    store_sem,
     gather_send,
     gather_recv,
     reduce_send,
@@ -330,7 +330,6 @@
 
     for load in loads[4:8]:
         load.wait()
-    stores = []
 
     def finish(c):
         start, width = chunks[c]
@@ -339,13 +338,13 @@
         grad = grads[mine, cols] + whole_in[0, hops - 2, :, start : start + width]
         grad = grad + whole_in[1, hops - 2, :, start : start + width]
         new = adamw(param[:, cols], grad, moment[:, cols], second[:, cols])
-        param[:, cols], moment[:, cols], second[:, cols] = new
         if start < width_a:
             outs, at = (out_a, out_moment_a, out_second_a), pl.ds(start, width)
         else:
             outs, at = (out_b, out_moment_b, out_second_b), pl.ds(start - width_a, width)
+        outs[0][my_half, at], outs[1][:, at], outs[2][:, at] = new
         copy = pltpu.make_async_remote_copy(
-            src_ref=param.at[:, cols],
+            src_ref=outs[0].at[my_half, at],
             dst_ref=outs[0].at[my_half, at],
             send_sem=pair_send.at[c],
             recv_sem=pair_recv.at[c],
@@ -354,18 +353,11 @@
         )
         copy.start()
         sent.append(copy)
-        targets = (outs[0].at[my_half, at], outs[1].at[:, at], outs[2].at[:, at])
-        for i, (source, target) in enumerate(zip((param, moment, second), targets)):
-            store = pltpu.make_async_copy(source.at[:, cols], target, store_sem.at[c, i])
-            store.start()
-            stores.append(store)
         return copy
 
     pairs = [finish(c) for c in (0, last_c, *range(1, last_c))]
     for pair in pairs:
         pair.wait_recv()
-    for store in stores:
-        store.wait()
     for copy in sent:
         copy.wait_send()
 
@@ -397,15 +389,15 @@
     results = pl.pallas_call(
         functools.partial(ring_kernel, n, chunks),
         out_shape=(
-            like(factor_a.shape, f32),
-            like(factor_b.shape, f32),
-            like((own, width_a), f32),
-            like((own, width_a), f32),
-            like((own, width_b), f32),
-            like((own, width_b), f32),
+            pltpu.VMEM(factor_a.shape, f32),
+            pltpu.VMEM(factor_b.shape, f32),
+            pltpu.VMEM((own, width_a), f32),
+            pltpu.VMEM((own, width_a), f32),
+            pltpu.VMEM((own, width_b), f32),
+            pltpu.VMEM((own, width_b), f32),
         ),
         in_specs=[HBM] * 10,
-        out_specs=(ANY,) * 6,
+        out_specs=(VMEM,) * 6,
         scratch_shapes=[
             pltpu.VMEM((toks, width_a), bf16),
             pltpu.VMEM((toks, width_b), bf16),
@@ -423,7 +415,6 @@
             pltpu.SMEM(args[8].shape, jnp.int32),
             pltpu.SMEM(args[9].shape, jnp.int32),
             dma((10,)),
-            dma((count, 3)),
             dma((3, 2, hops)),
             dma((3, 2, hops)),
             dma((count, 2, hops)),
@@ -432,13 +423,13 @@
             dma((count,)),
         ],
         compiler_params=pltpu.CompilerParams(
-            collective_id=0, has_side_effects=True, vmem_limit_bytes=63 << 20
+            collective_id=0, has_side_effects=True, vmem_limit_bytes=50 << 20
         ),
-    )(*args)
+    )(*(pltpu.with_memory_space_constraint(arg, pltpu.HBM) for arg in args))
     return pl.pallas_call(
         hand_out,
         out_shape=tuple(like(r.shape, r.dtype) for r in results),
-        in_specs=[ANY] * 6,
+        in_specs=[VMEM] * 6,
         out_specs=(HBM,) * 6,
         scratch_shapes=[dma((6,))],
     )(*results)

time: 105 us -> 62.6 us (0.60)
  Pallas kernels: 104 us -> 57.6 us
  local copies, waits for them, and re-layouts: 0 us -> 4.18 us
    pallas_call x1, Pallas kernels: 48.8 us -> 2.52 us  [local_ring(): pl.pallas_call(hand_out, out_shape=tuple((like(r.shape, r.dtype) for r in...]
    unnamed x0 -> x12, local copies, waits for them, and re-layouts: none -> 4.18 us
where the time goes in v3:
time: 62.6 us; the launch traced here: 62.4 us
  Pallas kernels  57.6 us (92%)
  local copies, waits for them, and re-layouts  4.18 us (7%)
  between operations  0.66 us (1%)
    pallas_call x1, Pallas kernels, local_ring(): pl.pallas_call(functools.partial(ring_kernel, n, chunks), out_shape=(pltp...  55.1 us
    unnamed x12, local copies, waits for them, and re-layouts  4.18 us
    pallas_call x1, Pallas kernels, local_ring(): pl.pallas_call(hand_out, out_shape=tuple((like(r.shape, r.dtype) for r in...  2.52 us

profile of v3, /device:TPU:0, one launch (start us, length us, event | category | flops | bytes accessed | tf_op | source)
XLA Modules:
  0.0 62.4 jit_solution(11131255375384408397)
XLA Ops:
  0.6 55.1 %shard_map.145 = (f32[32,5120]{1,0:T(8,128)S(1)}, f32[32,1024]{1,0:T(8,128)S(1)}, f32[16,5120]{1,0:T(8,128)S(1)}, f32[16,5120]{1,0:T(8,128)S(1)}, f32[16,1024]{1,0:T(8,128)S(1)}, /*index=5*/f32[16,1024]{1,0:T(8,128)S(1)}) custom-call(bf16[1024,5120]{1,0:T(8,128)(2,1)} %tokens.1, bf16[1024,1024]{1,0:T(8,128)(2,1)} %cotangent.1, f32[32,5120]{1,0:T(8,128)} %factor_a.1, ...), custom_call_target="tpu_custom_call" | custom-call | tf_op jit(solution)/shard_map/pallas_call | solution.py:389
  55.7 0.0 copy-start
  55.7 0.8 %copy-done = f32[32,5120]{1,0:T(8,128)} copy-done((f32[32,5120]{1,0:T(8,128)}, f32[32,5120]{1,0:T(8,128)S(1)}, u32[]{:S(2)}) %copy-start) | copy-done | bytes 655384
  56.5 0.0 copy-start.1
  56.5 0.7 %copy-done.1 = f32[16,5120]{1,0:T(8,128)} copy-done((f32[16,5120]{1,0:T(8,128)}, f32[16,5120]{1,0:T(8,128)S(1)}, u32[]{:S(2)}) %copy-start.1) | copy-done | bytes 327704
  57.3 0.0 copy-start.2
  57.3 0.7 %copy-done.2 = f32[16,5120]{1,0:T(8,128)} copy-done((f32[16,5120]{1,0:T(8,128)}, f32[16,5120]{1,0:T(8,128)S(1)}, u32[]{:S(2)}) %copy-start.2) | copy-done | bytes 327704
  58.0 0.0 copy-start.3
  58.0 0.7 %copy-done.3 = f32[32,1024]{1,0:T(8,128)} copy-done((f32[32,1024]{1,0:T(8,128)}, f32[32,1024]{1,0:T(8,128)S(1)}, u32[]{:S(2)}) %copy-start.3) | copy-done | bytes 131096
  58.6 0.0 copy-start.4
  58.7 0.6 copy-done.4
  59.3 0.0 copy-start.5
  59.3 0.6 copy-done.5
  59.9 2.5 %shard_map.146 = (f32[32,5120]{1,0:T(8,128)}, f32[32,1024]{1,0:T(8,128)}, f32[16,5120]{1,0:T(8,128)}, f32[16,5120]{1,0:T(8,128)}, f32[16,1024]{1,0:T(8,128)}, /*index=5*/f32[16,1024]{1,0:T(8,128)}) custom-call(f32[32,5120]{1,0:T(8,128)} %copy-done, f32[32,1024]{1,0:T(8,128)} %copy-done.3, f32[16,5120]{1,0:T(8,128)} %copy-done.1, f32[16,5120]{1,0:T(8,128)} %copy-done.2, ...), custom_call_target="tpu_custom_call" | custom-call | tf_op jit(solution)/shard_map/pallas_call | solution.py:429
Async XLA Ops:
  55.7 0.8 %copy-start = (f32[32,5120]{1,0:T(8,128)}, f32[32,5120]{1,0:T(8,128)S(1)}, u32[]{:S(2)}) copy-start(f32[32,5120]{1,0:T(8,128)S(1)} %get-tuple-element.12.refs_0_) | copy-start | bytes 1966084
  56.5 0.7 %copy-start.1 = (f32[16,5120]{1,0:T(8,128)}, f32[16,5120]{1,0:T(8,128)S(1)}, u32[]{:S(2)}) copy-start(f32[16,5120]{1,0:T(8,128)S(1)} %get-tuple-element.14.refs_2_) | copy-start | bytes 983044
  57.3 0.7 %copy-start.2 = (f32[16,5120]{1,0:T(8,128)}, f32[16,5120]{1,0:T(8,128)S(1)}, u32[]{:S(2)}) copy-start(f32[16,5120]{1,0:T(8,128)S(1)} %get-tuple-element.15.refs_3_) | copy-start | bytes 983044
  58.0 0.7 %copy-start.3 = (f32[32,1024]{1,0:T(8,128)}, f32[32,1024]{1,0:T(8,128)S(1)}, u32[]{:S(2)}) copy-start(f32[32,1024]{1,0:T(8,128)S(1)} %get-tuple-element.13.refs_1_) | copy-start | bytes 393220
  58.6 0.6 copy-start.4
  59.3 0.6 copy-start.5

commit v4 on v3

--- a/solution.py
+++ b/solution.py
@@ -299,34 +299,30 @@
         reduce_step(c, 1)
         if c < 2:
             gather(c, hops)
-    for c in range(last_c):
-        reduce_step(c, 2)
-    gather(0, hops + 1)
-    gather(1, hops + 1)
-
-    depth = 1024
-    scores[...] = jnp.zeros_like(scores)
-
-    def score_tile(i, carry):
-        cols = pl.ds(pl.multiple_of(i * depth, depth), depth)
-        scores[...] += lax.dot_general(
-            low_a[:, cols], tok[:, cols], last, preferred_element_type=jnp.float32
+    def score(start, width, first):
+        term = lax.dot_general(
+            low_a[:, start : start + width],
+            tok[:, start : start + width],
+            last,
+            preferred_element_type=jnp.float32,
         )
-        return carry
-
-    lax.fori_loop(0, width_a // depth, score_tile, 0)
+        scores[...] = term if first else scores[...] + term
+
+    later = [(c, t) for t in range(2, hops + 1) for c in range(last_c)]
+    for c, (start, width) in enumerate(chunks[:last_c]):
+        if c % 2 == 0:
+            gather(c // 2, hops + 1)
+        score(start, width, c == 0)
+        for _ in range(2 if c == 0 else 1):
+            reduce_step(*later.pop(0))
     hidden[...] = jnp.where(same, scores[...], 0.0).astype(jnp.bfloat16)
     grads[:, cols_b] = jnp.dot(hidden[...], cot[...], preferred_element_type=jnp.float32)
-    reduce_step(last_c, 1)
-    middle = last_c // 2
-    reduce_step(0, 3)
-    reduce_step(last_c, 2)
-    for t in range(3, hops + 1):
-        for c in range(last_c):
-            if (c, t) != (0, 3):
-                reduce_step(c, t)
-            if c == middle:
-                reduce_step(last_c, t)
+    t = 1
+    while later:
+        if t <= hops:
+            reduce_step(last_c, t)
+            t += 1
+        reduce_step(*later.pop(0))
 
     for load in loads[4:8]:
         load.wait()
@@ -432,6 +428,7 @@
         in_specs=[VMEM] * 6,
         out_specs=(HBM,) * 6,
         scratch_shapes=[dma((6,))],
+        compiler_params=pltpu.CompilerParams(vmem_limit_bytes=4 << 20),
     )(*results)
 
 

time: 62.6 us -> 58.3 us (0.931)
  local copies, waits for them, and re-layouts: 4.18 us -> 0 us
    unnamed x12 -> x0, local copies, waits for them, and re-layouts: 4.18 us -> none
    pallas_call x1, Pallas kernels: 2.52 us -> 1.18 us  [local_ring(): pl.pallas_call(hand_out, out_shape=tuple((like(r.shape, r.dtype) for r in...]
    pallas_call x1, Pallas kernels: 55.1 us -> 56.3 us  [local_ring(): pl.pallas_call(functools.partial(ring_kernel, n, chunks), out_shape=(pltp...]
where the time goes in v4:
time: 58.3 us; the launch traced here: 58.2 us
  Pallas kernels  57.5 us (99%)
  between operations  0.64 us (1%)
    pallas_call x1, Pallas kernels, local_ring(): pl.pallas_call(functools.partial(ring_kernel, n, chunks), out_shape=(pltp...  56.3 us
    pallas_call x1, Pallas kernels, local_ring(): pl.pallas_call(hand_out, out_shape=tuple((like(r.shape, r.dtype) for r in...  1.18 us

profile of v4, /device:TPU:0, one launch (start us, length us, event | category | flops | bytes accessed | tf_op | source)
XLA Modules:
  0.0 58.2 jit_solution(16174758566041232260)
XLA Ops:
  0.6 56.3 %shard_map.145 = (f32[32,5120]{1,0:T(8,128)S(1)}, f32[32,1024]{1,0:T(8,128)S(1)}, f32[16,5120]{1,0:T(8,128)S(1)}, f32[16,5120]{1,0:T(8,128)S(1)}, f32[16,1024]{1,0:T(8,128)S(1)}, /*index=5*/f32[16,1024]{1,0:T(8,128)S(1)}) custom-call(bf16[1024,5120]{1,0:T(8,128)(2,1)} %tokens.1, bf16[1024,1024]{1,0:T(8,128)(2,1)} %cotangent.1, f32[32,5120]{1,0:T(8,128)} %factor_a.1, ...), custom_call_target="tpu_custom_call" | custom-call | tf_op jit(solution)/shard_map/pallas_call | solution.py:385
  57.0 1.2 %shard_map.146 = (f32[32,5120]{1,0:T(8,128)}, f32[32,1024]{1,0:T(8,128)}, f32[16,5120]{1,0:T(8,128)}, f32[16,5120]{1,0:T(8,128)}, f32[16,1024]{1,0:T(8,128)}, /*index=5*/f32[16,1024]{1,0:T(8,128)}) custom-call(f32[32,5120]{1,0:T(8,128)S(1)} %get-tuple-element.12.refs_0_, f32[32,1024]{1,0:T(8,128)S(1)} %get-tuple-element.13.refs_1_, ...), custom_call_target="tpu_custom_call" | custom-call | tf_op jit(solution)/shard_map/pallas_call | solution.py:425

commit v5 on v4

--- a/solution.py
+++ b/solution.py
@@ -297,8 +297,7 @@
             back[...], tok[:, start : start + width], preferred_element_type=jnp.float32
         )
         reduce_step(c, 1)
-        if c < 2:
-            gather(c, hops)
+        gather(c, hops)
     def score(start, width, first):
         term = lax.dot_general(
             low_a[:, start : start + width],
@@ -310,19 +309,18 @@
 
     later = [(c, t) for t in range(2, hops + 1) for c in range(last_c)]
     for c, (start, width) in enumerate(chunks[:last_c]):
-        if c % 2 == 0:
-            gather(c // 2, hops + 1)
+        reduce_step(*later.pop(0))
+        gather(c, hops + 1)
         score(start, width, c == 0)
-        for _ in range(2 if c == 0 else 1):
-            reduce_step(*later.pop(0))
     hidden[...] = jnp.where(same, scores[...], 0.0).astype(jnp.bfloat16)
     grads[:, cols_b] = jnp.dot(hidden[...], cot[...], preferred_element_type=jnp.float32)
     t = 1
-    while later:
+    while later or t <= hops:
         if t <= hops:
             reduce_step(last_c, t)
             t += 1
-        reduce_step(*later.pop(0))
+        if later:
+            reduce_step(*later.pop(0))
 
     for load in loads[4:8]:
         load.wait()
@@ -376,8 +374,8 @@
     width = width_a + width_b
     rows = n * own
     hops = n // 2
-    part = width_a // 4
-    chunks = (*((i * part, part) for i in range(4)), (width_a, width_b))
+    part = width_a // 2
+    chunks = (*((i * part, part) for i in range(2)), (width_a, width_b))
     f32, bf16 = jnp.float32, jnp.bfloat16
     count = len(chunks)
     dma = pltpu.SemaphoreType.DMA

time: 58.3 us -> 56.4 us (0.967)
  Pallas kernels: 57.5 us -> 55.6 us
    pallas_call x1, Pallas kernels: 56.3 us -> 54.4 us  [local_ring(): pl.pallas_call(functools.partial(ring_kernel, n, chunks), out_shape=(pltp...]
where the time goes in v5:
time: 56.4 us; the launch traced here: 56.2 us
  Pallas kernels  55.6 us (99%)
  between operations  0.64 us (1%)
    pallas_call x1, Pallas kernels, local_ring(): pl.pallas_call(functools.partial(ring_kernel, n, chunks), out_shape=(pltp...  54.4 us
    pallas_call x1, Pallas kernels, local_ring(): pl.pallas_call(hand_out, out_shape=tuple((like(r.shape, r.dtype) for r in...  1.18 us

profile of v5, /device:TPU:0, one launch (start us, length us, event | category | flops | bytes accessed | tf_op | source)
XLA Modules:
  0.0 56.2 jit_solution(7201523947322795220)
XLA Ops:
  0.6 54.4 %shard_map.145 = (f32[32,5120]{1,0:T(8,128)S(1)}, f32[32,1024]{1,0:T(8,128)S(1)}, f32[16,5120]{1,0:T(8,128)S(1)}, f32[16,5120]{1,0:T(8,128)S(1)}, f32[16,1024]{1,0:T(8,128)S(1)}, /*index=5*/f32[16,1024]{1,0:T(8,128)S(1)}) custom-call(bf16[1024,5120]{1,0:T(8,128)(2,1)} %tokens.1, bf16[1024,1024]{1,0:T(8,128)(2,1)} %cotangent.1, f32[32,5120]{1,0:T(8,128)} %factor_a.1, ...), custom_call_target="tpu_custom_call" | custom-call | tf_op jit(solution)/shard_map/pallas_call | solution.py:383
  55.0 1.2 %shard_map.146 = (f32[32,5120]{1,0:T(8,128)}, f32[32,1024]{1,0:T(8,128)}, f32[16,5120]{1,0:T(8,128)}, f32[16,5120]{1,0:T(8,128)}, f32[16,1024]{1,0:T(8,128)}, /*index=5*/f32[16,1024]{1,0:T(8,128)}) custom-call(f32[32,5120]{1,0:T(8,128)S(1)} %get-tuple-element.12.refs_0_, f32[32,1024]{1,0:T(8,128)S(1)} %get-tuple-element.13.refs_1_, ...), custom_call_target="tpu_custom_call" | custom-call | tf_op jit(solution)/shard_map/pallas_call | solution.py:423
